TPU v7x, 256 devices: a whole 4x4x8 slice. The times are simulated.
256 devices in a mesh: fluid: 64 (over x, z, core), metal: 4 (over y).
Axes of the slice: x: 4, y: 4, z: 8, core: 2. Of those that a mesh axis runs over, the one named last changes fastest.
Arguments:
- fluid_x: bfloat16 [16384, 512], P('fluid', 'metal'), may hold values from -32 to 32
- metal_x: bfloat16 [8192, 512], P('fluid', 'metal'), may hold values from -32 to 32
- w_rf: bfloat16 [512, 512], P(None, 'metal'), may hold values from -0.5 to 0.5
- w_vf: bfloat16 [512, 512], P(None, 'metal'), may hold values from -0.25 to 0.25
- w_rm: bfloat16 [512, 512], P(None, 'metal'), may hold values from -0.5 to 0.5
- w_vm: bfloat16 [512, 512], P(None, 'metal'), may hold values from -0.25 to 0.25
- fluid_grad: bfloat16 [16384, 512], P('fluid', 'metal'), may hold values from -6 to 6
- metal_grad: bfloat16 [8192, 512], P('fluid', 'metal'), may hold values from -6 to 6
- pair_list: int32 [2048, 2], P('fluid'), may hold values from 0 to 63, as said below
- pair_count: int32 [64], P('fluid'), may hold values from 2 to 32, as said below
Outputs:
- fluid_out: bfloat16 [16384, 512], P('fluid', 'metal')
- metal_out: bfloat16 [8192, 512], P('fluid', 'metal')
- fluid_dx: bfloat16 [16384, 512], P('fluid', 'metal')
- metal_dx: bfloat16 [8192, 512], P('fluid', 'metal')
- weight_grads: float32 [4, 512, 512], P(None, None, 'metal')
Inputs may be any that keep to these rules, and one draw needn't show every extreme that they name: `pair_list`: column 0 is a local fluid block below 2, column 1 a metal block below 64. The first pair_count[d] entries of fluid index d are distinct pairs; every fluid block of every index and every metal block stands in some live entry; entries past the count hold valid indices and are ignored. `pair_count`: some fluid index has all 32 slots live.
All inputs are finite; a program needn't handle non-finite values.
Results may differ from a plain program's by a relative error of at most 0.0179.
The roundings to bfloat16 on the way count: a program that leaves them out, or rounds other values in their place, can miss the bound.
Values may be sent and summed in bfloat16 or wider, within the bound.
No kernel may reach another device: no remote copies, remote signals or barrier semaphores. Data moves between devices by JAX's collectives and lax.ppermute only.
A program may use at most 128 MiB of HBM per device.

v0:
```python
import math
import jax
import jax.numpy as jnp
from jax import lax
from jax.sharding import PartitionSpec as P

D = 512
H = 8
BLK = 128
LOWEST = -1e30


def project(inputs, weight):
    return jnp.dot(inputs, weight, preferred_element_type=jnp.float32).astype(jnp.bfloat16)


def back_project(grads, weight):
    return lax.dot_general(
        grads, weight, (((1,), (1,)), ((), ())), preferred_element_type=jnp.float32
    )


def outer_rows(inputs, grads):
    return lax.dot_general(
        inputs, grads, (((0,), (0,)), ((), ())), preferred_element_type=jnp.float32
    )


def body(fluid_x, metal_x, w_rf, w_vf, w_rm, w_vm, fluid_grad, metal_grad, pair_list, pair_count):
    head_size = D // H
    local_heads = w_rf.shape[1] // head_size
    feature_cols = w_rf.shape[1]
    fluid_rows = fluid_x.shape[0]
    blocks = fluid_rows // BLK
    metal_blocks = lax.axis_size("fluid")
    metal_rows = metal_blocks * BLK
    slot_total = pair_list.shape[0]
    batch_size = math.gcd(slot_total, 16)
    inv_root = 1.0 / math.sqrt(head_size)
    live_count = pair_count[0]
    loop_turns = slot_total // batch_size
    fluid_full, metal_full = (
        lax.all_gather(fluid_x, "metal", axis=1, tiled=True),
        lax.all_gather(metal_x, "metal", axis=1, tiled=True),
    )
    fluid_keys = project(fluid_full, w_rf)
    fluid_values = project(fluid_full, w_vf)
    metal_keys = project(metal_full, w_rm)
    metal_values = project(metal_full, w_vm)
    keys_all, values_all = (
        lax.all_gather(metal_keys, "fluid", axis=0, tiled=True),
        lax.all_gather(metal_values, "fluid", axis=0, tiled=True),
    )
    fkey_tiles = fluid_keys.reshape(blocks, BLK, local_heads, head_size)
    fval_tiles = fluid_values.reshape(blocks, BLK, local_heads, head_size)
    mkey_tiles = keys_all.reshape(metal_blocks, BLK, local_heads, head_size)
    mval_tiles = values_all.reshape(metal_blocks, BLK, local_heads, head_size)

    def batch_pairs(number):
        entries = lax.dynamic_slice_in_dim(pair_list, number * batch_size, batch_size, 0)
        slot_index = number * batch_size + jnp.arange(batch_size, dtype=jnp.int32)
        frows = entries[:, 0]
        mrows = entries[:, 1]
        scores = (
            jnp.einsum(
                "pahd,pbhd->phab",
                fkey_tiles[frows],
                mkey_tiles[mrows],
                preferred_element_type=jnp.float32,
            )
            * inv_root
        )
        return (frows, mrows, slot_index < live_count, scores)

    def max_pass(number, state):
        row_max, col_max = state
        frows, mrows, active, scores = batch_pairs(number)
        live = active[:, None, None]
        row_max = row_max.at[frows].max(jnp.where(live, jnp.max(scores, axis=3), LOWEST))
        col_max = col_max.at[mrows].max(jnp.where(live, jnp.max(scores, axis=2), LOWEST))
        return (row_max, col_max)

    row_max, col_local = lax.fori_loop(
        0,
        loop_turns,
        max_pass,
        (
            jnp.full((blocks, local_heads, BLK), LOWEST, jnp.float32),
            jnp.full((metal_blocks, local_heads, BLK), LOWEST, jnp.float32),
        ),
    )
    col_max = lax.pmax(col_local, "fluid")

    def sum_pass(number, state):
        row_sum, fluid_num, col_sum, metal_num = state
        frows, mrows, active, scores = batch_pairs(number)
        live = active[:, None, None, None]
        row_exp = jnp.where(live, jnp.exp(scores - row_max[frows][:, :, :, None]), 0.0)
        col_exp = jnp.where(live, jnp.exp(scores - col_max[mrows][:, :, None, :]), 0.0)
        row_sum = row_sum.at[frows].add(jnp.sum(row_exp, axis=3))
        col_sum = col_sum.at[mrows].add(jnp.sum(col_exp, axis=2))
        fluid_num = fluid_num.at[frows].add(
            jnp.einsum(
                "phab,pbhd->pahd",
                row_exp.astype(jnp.bfloat16),
                mval_tiles[mrows],
                preferred_element_type=jnp.float32,
            )
        )
        metal_num = metal_num.at[mrows].add(
            jnp.einsum(
                "phab,pahd->pbhd",
                col_exp.astype(jnp.bfloat16),
                fval_tiles[frows],
                preferred_element_type=jnp.float32,
            )
        )
        return (row_sum, fluid_num, col_sum, metal_num)

    row_sum, fluid_num, col_sum, metal_num = lax.fori_loop(
        0,
        loop_turns,
        sum_pass,
        (
            jnp.zeros((blocks, local_heads, BLK), jnp.float32),
            jnp.zeros((blocks, BLK, local_heads, head_size), jnp.float32),
            jnp.zeros((metal_blocks, local_heads, BLK), jnp.float32),
            jnp.zeros((metal_blocks, BLK, local_heads, head_size), jnp.float32),
        ),
    )
    fluid_out = (
        (fluid_num / row_sum.transpose(0, 2, 1)[:, :, :, None])
        .reshape(fluid_rows, feature_cols)
        .astype(jnp.bfloat16)
    )
    num_rows = metal_num.reshape(metal_rows, feature_cols)
    total_rows = col_sum.transpose(0, 2, 1).reshape(metal_rows, local_heads)
    own_num, own_sum = (
        lax.psum_scatter(num_rows, "fluid", scatter_dimension=0, tiled=True),
        lax.psum_scatter(total_rows, "fluid", scatter_dimension=0, tiled=True),
    )
    metal_out = (
        (own_num.reshape(BLK, local_heads, head_size) / own_sum[:, :, None])
        .reshape(BLK, feature_cols)
        .astype(jnp.bfloat16)
    )
    scaled_grad = (
        (metal_grad.astype(jnp.float32).reshape(BLK, local_heads, head_size) / own_sum[:, :, None])
        .reshape(BLK, feature_cols)
        .astype(jnp.bfloat16)
    )
    scaled_all, output_all = (
        lax.all_gather(scaled_grad, "fluid", axis=0, tiled=True),
        lax.all_gather(metal_out, "fluid", axis=0, tiled=True),
    )
    delta_f = jnp.sum(
        (fluid_grad.astype(jnp.float32) * fluid_out.astype(jnp.float32)).reshape(
            fluid_rows, local_heads, head_size
        ),
        axis=2,
    )
    delta_m = jnp.sum(
        (scaled_all.astype(jnp.float32) * output_all.astype(jnp.float32)).reshape(
            metal_blocks, BLK, local_heads, head_size
        ),
        axis=3,
    )
    grad_tiles = fluid_grad.reshape(blocks, BLK, local_heads, head_size)
    scaled_tiles = scaled_all.reshape(metal_blocks, BLK, local_heads, head_size)
    dfluid_tiles = delta_f.reshape(blocks, BLK, local_heads)

    def grad_pass(number, state):
        grad_rf, grad_vf, grad_rm, grad_vm = state
        frows, mrows, active, scores = batch_pairs(number)
        live = active[:, None, None, None]
        attn = jnp.where(
            live,
            jnp.exp(scores - row_max[frows][:, :, :, None]) / row_sum[frows][:, :, :, None],
            0.0,
        )
        col_exp = jnp.where(live, jnp.exp(scores - col_max[mrows][:, :, None, :]), 0.0)
        fluid_term = jnp.einsum(
            "pahd,pbhd->phab",
            grad_tiles[frows],
            mval_tiles[mrows],
            preferred_element_type=jnp.float32,
        )
        metal_term = jnp.einsum(
            "pahd,pbhd->phab",
            fval_tiles[frows],
            scaled_tiles[mrows],
            preferred_element_type=jnp.float32,
        )
        dscore = attn * (fluid_term - dfluid_tiles[frows].transpose(0, 2, 1)[:, :, :, None])
        dscore = dscore + col_exp * (metal_term - delta_m[mrows].transpose(0, 2, 1)[:, :, None, :])
        dscore_weight = dscore.astype(jnp.bfloat16)
        grad_rf = grad_rf.at[frows].add(
            jnp.einsum(
                "phab,pbhd->pahd",
                dscore_weight,
                mkey_tiles[mrows],
                preferred_element_type=jnp.float32,
            )
            * inv_root
        )
        grad_vf = grad_vf.at[frows].add(
            jnp.einsum(
                "phab,pbhd->pahd",
                col_exp.astype(jnp.bfloat16),
                scaled_tiles[mrows],
                preferred_element_type=jnp.float32,
            )
        )
        grad_rm = grad_rm.at[mrows].add(
            jnp.einsum(
                "phab,pahd->pbhd",
                dscore_weight,
                fkey_tiles[frows],
                preferred_element_type=jnp.float32,
            )
            * inv_root
        )
        grad_vm = grad_vm.at[mrows].add(
            jnp.einsum(
                "phab,pahd->pbhd",
                attn.astype(jnp.bfloat16),
                grad_tiles[frows],
                preferred_element_type=jnp.float32,
            )
        )
        return (grad_rf, grad_vf, grad_rm, grad_vm)

    grad_rf, grad_vf, grad_rm, grad_vm = lax.fori_loop(
        0,
        loop_turns,
        grad_pass,
        (
            jnp.zeros((blocks, BLK, local_heads, head_size), jnp.float32),
            jnp.zeros((blocks, BLK, local_heads, head_size), jnp.float32),
            jnp.zeros((metal_blocks, BLK, local_heads, head_size), jnp.float32),
            jnp.zeros((metal_blocks, BLK, local_heads, head_size), jnp.float32),
        ),
    )
    rf_rounded = grad_rf.reshape(fluid_rows, feature_cols).astype(jnp.bfloat16)
    vf_rounded = grad_vf.reshape(fluid_rows, feature_cols).astype(jnp.bfloat16)
    fluid_part = back_project(rf_rounded, w_rf) + back_project(vf_rounded, w_vf)
    fluid_part, weight_rf, weight_vf = (
        fluid_part,
        outer_rows(fluid_full, rf_rounded),
        outer_rows(fluid_full, vf_rounded),
    )
    rm_rounded = lax.psum_scatter(
        grad_rm.reshape(metal_rows, feature_cols), "fluid", scatter_dimension=0, tiled=True
    ).astype(jnp.bfloat16)
    vm_rounded = lax.psum_scatter(
        grad_vm.reshape(metal_rows, feature_cols), "fluid", scatter_dimension=0, tiled=True
    ).astype(jnp.bfloat16)
    metal_part = back_project(rm_rounded, w_rm) + back_project(vm_rounded, w_vm)
    weight_rm = outer_rows(metal_full, rm_rounded)
    weight_vm = outer_rows(metal_full, vm_rounded)
    fluid_dx, metal_dx = (
        lax.psum_scatter(fluid_part, "metal", scatter_dimension=1, tiled=True),
        lax.psum_scatter(metal_part, "metal", scatter_dimension=1, tiled=True),
    )
    weight_grads = lax.psum(jnp.stack([weight_rf, weight_vf, weight_rm, weight_vm]), "fluid")
    return (
        fluid_out,
        metal_out,
        fluid_dx.astype(jnp.bfloat16),
        metal_dx.astype(jnp.bfloat16),
        weight_grads,
    )


def solution(mesh):
    placed = (
        P("fluid", "metal"),
        P("fluid", "metal"),
        P(None, "metal"),
        P(None, "metal"),
        P(None, "metal"),
        P(None, "metal"),
        P("fluid", "metal"),
        P("fluid", "metal"),
        P("fluid", None),
        P("fluid"),
    )
    return jax.shard_map(
        body,
        mesh=mesh,
        in_specs=placed,
        out_specs=(
            P("fluid", "metal"),
            P("fluid", "metal"),
            P("fluid", "metal"),
            P("fluid", "metal"),
            P(None, None, "metal"),
        ),
        check_vma=False,
    )
```

profile of v0, /device:TPU:2, one launch (start us, length us, event | category | flops | bytes accessed | tf_op | source)
XLA Modules:
  0.0 1555.2 jit_solution(13822160661187020611)
XLA Ops:
  7.2 11.8 all_gather.19
  22.6 11.7 all_gather.18
  34.7 64.7 %all-gather.5.cloned.1.call-done = bf16[8192,128]{1,0:T(8,128)(2,1)} async-done(((bf16[128,128]{1,0:T(8,128)(2,1)}), bf16[8192,128]{1,0:T(8,128)(2,1)}) %all-gather.5.cloned.1.call-update) | async-done | bytes 2097168 | tf_op jit(solution)/shard_map/all_gather | solution.py:51
  99.4 8.2 reshape.334
  107.6 23.2 %while.53 = (s32[]{:T(128)}, f32[2,2,128]{2,1,0:T(2,128)S(1)}, f32[64,2,128]{2,1,0:T(2,128)S(1)}, s32[32,2]{0,1:T(2,128)S(1)}, s32[]{:T(128)}, /*index=5*/bf16[2...) while((s32[]{:T(128)}, f32[2,2,128]{2,1,0:T(2,128)S(1)}, ...), condition=%wide.region_5.6_spmd, body=%wide.region_0.5_spmd.sunk | while | flops 68692104 | bytes 3351623 | solution.py:83
  131.9 45.8 %all-gather.7.cloned.1.call-done = bf16[8192,128]{1,0:T(8,128)(2,1)} async-done(((bf16[128,128]{1,0:T(8,128)(2,1)}), bf16[8192,128]{1,0:T(8,128)(2,1)}) %all-gather.7.cloned.1.call-update) | async-done | bytes 2097168 | tf_op jit(solution)/shard_map/all_gather | solution.py:52
  177.7 8.3 reshape.335
  185.9 161.9 %all-reduce.3.cloned.1.call-done = f32[64,2,128]{2,1,0:T(2,128)} async-done(((f32[64,2,128]{2,1,0:T(2,128)}), f32[64,2,128]{2,1,0:T(2,128)}) %all-reduce.3.cloned.1.call-update) | async-done | bytes 65552 | tf_op jit(solution)/shard_map/pmax | solution.py:92
  350.3 67.5 %while.54 = (s32[]{:T(128)}, f32[2,2,128]{2,1,0:T(2,128)S(1)}, f32[2,128,2,64]{1,3,2,0:T(8,128)S(1)}, f32[64,2,128]{2,1,0:T(2,128)S(1)}, f32[64,128,2,64]{1,3,2,...) while((s32[]{:T(128)}, f32[2,2,128]{2,1,0:T(2,128)S(1)}, ...), condition=%wide.region_14.15_spmd, body=%wide.region_7.14_spmd.sunk | while | flops 209717376 | bytes 25437748 | solution.py:120
  358.2 5.7 gather_fusion.4
  391.6 5.7 gather_fusion.4
  431.3 130.0 %reduce-scatter.19.cloned.1.call-done = f32[128,2]{1,0:T(8,128)} async-done(((f32[8192,2]{1,0:T(8,128)}), f32[128,2]{1,0:T(8,128)}) %reduce-scatter.19.cloned.1.call-update) | async-done | bytes 1040
  562.2 145.2 %reduce-scatter.9.cloned.1.call-done = f32[128,128]{0,1:T(8,128)} async-done(((f32[8192,128]{0,1:T(8,128)}), f32[128,128]{0,1:T(8,128)}) %reduce-scatter.9.cloned.1.call-update) | async-done | bytes 65552 | tf_op jit(solution)/shard_map/reduce_scatter | solution.py:139
  710.1 72.3 %all-gather.9.cloned.1.call-done = bf16[8192,128]{0,1:T(8,128)(2,1)} async-done(((bf16[128,128]{0,1:T(8,128)(2,1)}), bf16[8192,128]{0,1:T(8,128)(2,1)}) %all-gather.9.cloned.1.call-update) | async-done | bytes 2097168 | tf_op jit(solution)/shard_map/all_gather | solution.py:153
  782.4 74.9 %all-gather.11.cloned.1.call-done = bf16[8192,128]{0,1:T(8,128)(2,1)} async-done(((bf16[128,128]{0,1:T(8,128)(2,1)}), bf16[8192,128]{0,1:T(8,128)(2,1)}) %all-gather.11.cloned.1.call-update) | async-done | bytes 2097168 | tf_op jit(solution)/shard_map/all_gather | solution.py:154
  877.5 131.7 %while.55 = (s32[]{:T(128)}, f32[2,128,2,64]{1,3,2,0:T(8,128)S(1)}, f32[2,128,2,64]{1,3,2,0:T(8,128)S(1)}, f32[64,128,2,64]{1,3,2,0:T(8,128)}, f32[64,128,2,64]{...) while((s32[]{:T(128)}, f32[2,128,2,64]{1,3,2,0:T(8,128)S(1)}, ...), condition=%wide.region_24.25_spmd, body=%wide.region_19.24_spmd.sunk | while | flops 482347136 | bytes 61189336 | solution.py:233
  895.4 5.7 gather_fusion.8
  961.1 5.7 gather_fusion.8
  1023.8 5.3 copy.185
  1031.5 129.8 %reduce-scatter.15.cloned.1.call-done = f32[128,128]{0,1:T(8,128)} async-done(((f32[8192,128]{0,1:T(8,128)}), f32[128,128]{0,1:T(8,128)}) %reduce-scatter.15.cloned.1.call-update) | async-done | bytes 65552 | tf_op jit(solution)/shard_map/reduce_scatter | solution.py:255
  1162.3 145.3 %reduce-scatter.13.cloned.1.call-done = f32[128,128]{0,1:T(8,128)} async-done(((f32[8192,128]{0,1:T(8,128)}), f32[128,128]{0,1:T(8,128)}) %reduce-scatter.13.cloned.1.call-update) | async-done | bytes 65552 | tf_op jit(solution)/shard_map/reduce_scatter | solution.py:252
  1312.6 20.7 %reduce-scatter.11.cloned.1.call-done = f32[256,128]{1,0:T(8,128)} async-done(((f32[256,512]{1,0:T(8,128)}), f32[256,128]{1,0:T(8,128)}) %reduce-scatter.11.cloned.1.call-update) | async-done | bytes 131088 | tf_op jit(solution)/shard_map/reduce_scatter | solution.py:262
  1334.8 188.6 %all-reduce.5.cloned.1.call-done = f32[4,512,128]{1,2,0:T(8,128)} async-done(((f32[4,512,128]{1,2,0:T(8,128)}), f32[4,512,128]{1,2,0:T(8,128)}) %all-reduce.5.cloned.1.call-update) | async-done | bytes 1048592 | tf_op jit(solution)/shard_map/psum | solution.py:265
  1525.9 20.6 %reduce-scatter.17.cloned.1.call-done = f32[128,128]{1,0:T(8,128)} async-done(((f32[128,512]{1,0:T(8,128)}), f32[128,128]{1,0:T(8,128)}) %reduce-scatter.17.cloned.1.call-update) | async-done | bytes 65552 | tf_op jit(solution)/shard_map/reduce_scatter | solution.py:263
  (269 shorter events, 270.7 us)
Async XLA Ops:
  7.2 27.2 %copy-start = (bf16[512,128]{1,0:T(8,128)(2,1)S(1)}, bf16[512,128]{1,0:T(8,128)(2,1)}, u32[]{:S(2)}) copy-start(bf16[512,128]{1,0:T(8,128)(2,1)} %param.18) | copy-start | bytes 393220
  7.2 92.2 %all-gather.5.cloned.1.call-start = ((), (), s32[]{:S(2)}) async-start(), calls=%async_computation.6 | async-start | bytes 2129920 | tf_op jit(solution)/shard_map/all_gather | solution.py:51
  19.0 15.3 copy-start.8
  20.8 156.9 %all-gather.7.cloned.1.call-start = ((), (), s32[]{:S(2)}) async-start(), calls=%async_computation.7 | async-start | bytes 2129920 | tf_op jit(solution)/shard_map/all_gather | solution.py:52
  22.6 325.3 %all-reduce.3.cloned.1.call-start = ((), (), s32[]{:S(2)}) async-start(), calls=%async_computation.8 | async-start | bytes 131072 | tf_op jit(solution)/shard_map/pmax | solution.py:92
  34.3 97.2 %copy-start.6 = (bf16[256,512]{1,0:T(8,128)(2,1)}, bf16[256,512]{1,0:T(8,128)(2,1)S(1)}, u32[]{:S(2)}) copy-start(bf16[256,512]{1,0:T(8,128)(2,1)S(1)} %all_gather.18) | copy-start | bytes 786436
  34.7 72.9 %copy-start.22 = (s32[32,2]{0,1:T(2,128)S(1)}, s32[32,2]{0,1:T(2,128)}, u32[]{:S(2)}) copy-start(s32[32,2]{0,1:T(2,128)} %param.24) | copy-start | bytes 772
  107.6 24.0 %copy-start.13 = (bf16[512,128]{1,0:T(8,128)(2,1)S(1)}, bf16[512,128]{1,0:T(8,128)(2,1)}, u32[]{:S(2)}) copy-start(bf16[512,128]{1,0:T(8,128)(2,1)} %param.19) | copy-start | bytes 393220
  131.5 429.8 %reduce-scatter.19.cloned.1.call-start = ((), (), s32[]{:S(2)}) async-start(), calls=%async_computation.17 | async-start | bytes 4259840
  410.1 3.9 copy-start.1
  420.5 286.9 %reduce-scatter.9.cloned.1.call-start = ((), (), s32[]{:S(2)}) async-start(), calls=%async_computation.9 | async-start | bytes 4259840 | tf_op jit(solution)/shard_map/reduce_scatter | solution.py:139
  430.4 279.3 %copy-start.20 = (bf16[256,128]{1,0:T(8,128)(2,1)S(1)}, bf16[256,128]{1,0:T(8,128)(2,1)}, u32[]{:S(2)}) copy-start(bf16[256,128]{1,0:T(8,128)(2,1)} %param.22) | copy-start | bytes 196612
  430.5 351.9 %all-gather.9.cloned.1.call-start = ((), (), s32[]{:S(2)}) async-start(), calls=%async_computation.10 | async-start | bytes 2129920 | tf_op jit(solution)/shard_map/all_gather | solution.py:153
  708.9 148.3 %all-gather.11.cloned.1.call-start = ((), (), s32[]{:S(2)}) async-start(), calls=%async_computation.11 | async-start | bytes 2129920 | tf_op jit(solution)/shard_map/all_gather | solution.py:154
  709.7 451.6 %reduce-scatter.15.cloned.1.call-start = ((), (), s32[]{:S(2)}) async-start(), calls=%async_computation.14 | async-start | bytes 4259840 | tf_op jit(solution)/shard_map/reduce_scatter | solution.py:255
  710.0 149.9 %copy-start.11 = (bf16[2,128,2,64]{1,0,3,2:T(2,128)(2,1)}, bf16[2,128,2,64]{1,0,3,2:T(2,128)(2,1)S(1)}, u32[]{:S(2)}) copy-start(bf16[2,128,2,64]{1,0,3,2:T(2,128)(2,1)S(1)} %copy.104) | copy-start | bytes 196612
  1019.1 288.5 %reduce-scatter.13.cloned.1.call-start = ((), (), s32[]{:S(2)}) async-start(), calls=%async_computation.13 | async-start | bytes 4259840 | tf_op jit(solution)/shard_map/reduce_scatter | solution.py:252
  1029.1 304.2 %reduce-scatter.11.cloned.1.call-start = ((), (), s32[]{:S(2)}) async-start(), calls=%async_computation.12 | async-start | bytes 655360 | tf_op jit(solution)/shard_map/reduce_scatter | solution.py:262
  1029.1 132.1 %copy-start.9 = (bf16[128,512]{1,0:T(8,128)(2,1)S(1)}, bf16[128,512]{1,0:T(8,128)(2,1)}, u32[]{:S(2)}) copy-start(bf16[128,512]{1,0:T(8,128)(2,1)} %copy-done.8) | copy-start | bytes 393220
  1031.0 492.3 %all-reduce.5.cloned.1.call-start = ((), (), s32[]{:S(2)}) async-start(), calls=%async_computation.16 | async-start | bytes 2097152 | tf_op jit(solution)/shard_map/psum | solution.py:265
  1031.5 278.4 %copy-start.15 = (bf16[512,128]{1,0:T(8,128)(2,1)S(1)}, bf16[512,128]{1,0:T(8,128)(2,1)}, u32[]{:S(2)}) copy-start(bf16[512,128]{1,0:T(8,128)(2,1)} %param.20) | copy-start | bytes 393220
  1162.3 147.8 %copy-start.16 = (bf16[512,128]{1,0:T(8,128)(2,1)S(1)}, bf16[512,128]{1,0:T(8,128)(2,1)}, u32[]{:S(2)}) copy-start(bf16[512,128]{1,0:T(8,128)(2,1)} %param.21) | copy-start | bytes 393220
  1162.3 147.8 %copy-start.21 = (f32[128,128]{0,1:T(8,128)S(1)}, f32[128,128]{0,1:T(8,128)}, u32[]{:S(2)}) copy-start(f32[128,128]{0,1:T(8,128)} %reduce-scatter.15.cloned.1.call-done) | copy-start | bytes 196612
  1309.8 236.7 %reduce-scatter.17.cloned.1.call-start = ((), (), s32[]{:S(2)}) async-start(), calls=%async_computation.15 | async-start | bytes 327680 | tf_op jit(solution)/shard_map/reduce_scatter | solution.py:263
  (28 other events, 49.7 us)
Sparse Core Ops, SparseCore 0:
  20.9 78.4 all-gather.4
  102.7 74.9 all-gather.6
  181.8 166.0 all-reduce.2
  420.7 140.5 reduce-scatter.18
  565.3 142.0 reduce-scatter.8
  710.7 71.6 all-gather.8
  785.8 71.3 all-gather.10
  1019.2 141.9 reduce-scatter.14
  1165.4 142.1 reduce-scatter.12
  1310.2 23.0 reduce-scatter.10
  1337.7 185.6 all-reduce.4
  1525.7 20.7 reduce-scatter.16
where the time goes:
time: 1570 us; the launch traced here: 1560 us
  waiting for transfers between devices  1200 us (76%)
  local copies, waits for them, and re-layouts  209 us (13%)
  other arithmetic  58.9 us (4%)
  matrix products  46.7 us (3%)
  blocking collectives  23.5 us (1%)
    psum x1, waiting for transfers between devices, body(): lax.psum(jnp.stack([weight_rf, weight_vf, weight_rm, weight_vm]), 'fluid')  189 us
    pmax x1, waiting for transfers between devices, body(): col_max = lax.pmax(col_local, 'fluid')  162 us
    reduce_scatter x1, waiting for transfers between devices, body(): lax.psum_scatter(grad_rm.reshape(metal_rows, feature_cols), 'fluid', scat...  145 us
    reduce_scatter x1, waiting for transfers between devices, body(): lax.psum_scatter(num_rows, 'fluid', scatter_dimension=0, tiled=True)  145 us
    unnamed x13, waiting for transfers between devices  131 us
    reduce_scatter x1, waiting for transfers between devices, body(): lax.psum_scatter(grad_vm.reshape(metal_rows, feature_cols), 'fluid', scat...  130 us
    all_gather x1, waiting for transfers between devices, body(): lax.all_gather(metal_out, 'fluid', axis=0, tiled=True)  74.9 us
    all_gather x1, waiting for transfers between devices, body(): lax.all_gather(scaled_grad, 'fluid', axis=0, tiled=True)  72.3 us
  transfers between devices with their start and end apart: 12, of which 12 were waited for; matrix products, arithmetic and copies ran while one was open for 5% of the time, Pallas kernels for 0%

commit v1 on v0

--- a/solution.py
+++ b/solution.py
@@ -3,6 +3,7 @@
 import jax.numpy as jnp
 from jax import lax
 from jax.sharding import PartitionSpec as P
+from jax.lax import all_to_all, axis_size
 
 D = 512
 H = 8
@@ -48,7 +49,15 @@
     metal_keys = project(metal_full, w_rm)
     metal_values = project(metal_full, w_vm)
     keys_all, values_all = (
-        lax.all_gather(metal_keys, "fluid", axis=0, tiled=True),
+        jnp.concatenate(
+            all_to_all(
+                jnp.stack([metal_keys for _ in range(axis_size("fluid"))], axis=0),
+                axis_name="fluid",
+                split_axis=0,
+                concat_axis=0,
+            ),
+            axis=0,
+        ),
         lax.all_gather(metal_values, "fluid", axis=0, tiled=True),
     )
     fkey_tiles = fluid_keys.reshape(blocks, BLK, local_heads, head_size)

time: 1570 us -> 1510 us (0.962)
  waiting for transfers between devices: 1200 us -> 1130 us
    all_gather x1 -> x0, waiting for transfers between devices: 64.7 us -> none  [body(): lax.all_gather(metal_keys, 'fluid', axis=0, tiled=True)]
    all_gather x1, waiting for transfers between devices: 45.8 us -> 1.53 us  [body(): lax.all_gather(metal_values, 'fluid', axis=0, tiled=True)]
    all_to_all x0 -> x1, waiting for transfers between devices: none -> 38.2 us  [body(): all_to_all(jnp.stack([metal_keys for _ in range(axis_size('fluid'))], axi...]
    unnamed x13 -> x12, waiting for transfers between devices: 131 us -> 131 us
where the time goes in v1:
time: 1510 us; the launch traced here: 1490 us
  waiting for transfers between devices  1130 us (75%)
  local copies, waits for them, and re-layouts  210 us (14%)
  other arithmetic  59 us (4%)
  matrix products  45.2 us (3%)
  blocking collectives  23.2 us (2%)
    psum x1, waiting for transfers between devices, body(): lax.psum(jnp.stack([weight_rf, weight_vf, weight_rm, weight_vm]), 'fluid')  188 us
    pmax x1, waiting for transfers between devices, body(): col_max = lax.pmax(col_local, 'fluid')  162 us
    reduce_scatter x1, waiting for transfers between devices, body(): lax.psum_scatter(grad_rm.reshape(metal_rows, feature_cols), 'fluid', scat...  145 us
    reduce_scatter x1, waiting for transfers between devices, body(): lax.psum_scatter(num_rows, 'fluid', scatter_dimension=0, tiled=True)  145 us
    unnamed x12, waiting for transfers between devices  131 us
    reduce_scatter x1, waiting for transfers between devices, body(): lax.psum_scatter(grad_vm.reshape(metal_rows, feature_cols), 'fluid', scat...  130 us
    all_gather x1, waiting for transfers between devices, body(): lax.all_gather(metal_out, 'fluid', axis=0, tiled=True)  74.7 us
    all_gather x1, waiting for transfers between devices, body(): lax.all_gather(scaled_grad, 'fluid', axis=0, tiled=True)  72.3 us
  transfers between devices with their start and end apart: 12, of which 12 were waited for; matrix products, arithmetic and copies ran while one was open for 5% of the time, Pallas kernels for 0%

profile of v1, /device:TPU:2, one launch (start us, length us, event | category | flops | bytes accessed | tf_op | source)
XLA Modules:
  0.0 1494.8 jit_solution(10302843328401554937)
XLA Ops:
  7.2 11.9 all_gather.16
  22.2 12.2 all-to-all-start
  35.3 11.3 all_gather.15
  46.9 38.2 %all-to-all-done = bf16[64,128,128]{1,2,0:T(8,128)(2,1)S(1)} async-done(((bf16[64,128,128]{1,2,0:T(8,128)(2,1)}), bf16[64,128,128]{1,2,0:T(8,128)(2,1)S(1)}, u32[]{:S(2)}, u32[]{:S(2)}) %all-to-all-start) | async-done | bytes 2097184 | tf_op jit(solution)/shard_map/all_to_all | solution.py:53
  85.2 7.4 copy.101
  92.6 23.3 %while.53 = (s32[]{:T(128)}, f32[2,2,128]{2,1,0:T(2,128)S(1)}, f32[64,2,128]{2,1,0:T(2,128)S(1)}, s32[32,2]{0,1:T(2,128)S(1)}, s32[]{:T(128)}, /*index=5*/bf16[2...) while((s32[]{:T(128)}, f32[2,2,128]{2,1,0:T(2,128)S(1)}, ...), condition=%wide.region_5.6_spmd, body=%wide.region_0.5_spmd.sunk | while | flops 68692104 | bytes 3351623 | solution.py:92
  118.5 8.3 reshape.332
  126.7 161.8 %all-reduce.3.cloned.1.call-done = f32[64,2,128]{2,1,0:T(2,128)} async-done(((f32[64,2,128]{2,1,0:T(2,128)}), f32[64,2,128]{2,1,0:T(2,128)}) %all-reduce.3.cloned.1.call-update) | async-done | bytes 65552 | tf_op jit(solution)/shard_map/pmax | solution.py:101
  291.0 67.5 %while.54 = (s32[]{:T(128)}, f32[2,2,128]{2,1,0:T(2,128)S(1)}, f32[2,128,2,64]{1,3,2,0:T(8,128)S(1)}, f32[64,2,128]{2,1,0:T(2,128)S(1)}, f32[64,128,2,64]{1,3,2,...) while((s32[]{:T(128)}, f32[2,2,128]{2,1,0:T(2,128)S(1)}, ...), condition=%wide.region_14.15_spmd, body=%wide.region_7.14_spmd.sunk | while | flops 209717376 | bytes 25437748 | solution.py:129
  298.8 5.7 gather_fusion.4
  332.3 5.7 gather_fusion.4
  372.0 130.1 %reduce-scatter.19.cloned.1.call-done = f32[128,2]{1,0:T(8,128)} async-done(((f32[8192,2]{1,0:T(8,128)}), f32[128,2]{1,0:T(8,128)}) %reduce-scatter.19.cloned.1.call-update) | async-done | bytes 1040
  502.9 145.3 %reduce-scatter.9.cloned.1.call-done = f32[128,128]{0,1:T(8,128)} async-done(((f32[8192,128]{0,1:T(8,128)}), f32[128,128]{0,1:T(8,128)}) %reduce-scatter.9.cloned.1.call-update) | async-done | bytes 65552 | tf_op jit(solution)/shard_map/reduce_scatter | solution.py:148
  650.7 72.3 %all-gather.6.cloned.1.call-done = bf16[8192,128]{0,1:T(8,128)(2,1)} async-done(((bf16[128,128]{0,1:T(8,128)(2,1)}), bf16[8192,128]{0,1:T(8,128)(2,1)}) %all-gather.6.cloned.1.call-update) | async-done | bytes 2097168 | tf_op jit(solution)/shard_map/all_gather | solution.py:162
  723.0 74.7 %all-gather.8.cloned.1.call-done = bf16[8192,128]{0,1:T(8,128)(2,1)} async-done(((bf16[128,128]{0,1:T(8,128)(2,1)}), bf16[8192,128]{0,1:T(8,128)(2,1)}) %all-gather.8.cloned.1.call-update) | async-done | bytes 2097168 | tf_op jit(solution)/shard_map/all_gather | solution.py:163
  818.0 131.7 %while.55 = (s32[]{:T(128)}, f32[2,128,2,64]{1,3,2,0:T(8,128)S(1)}, f32[2,128,2,64]{1,3,2,0:T(8,128)S(1)}, f32[64,128,2,64]{1,3,2,0:T(8,128)}, f32[64,128,2,64]{...) while((s32[]{:T(128)}, f32[2,128,2,64]{1,3,2,0:T(8,128)S(1)}, ...), condition=%wide.region_24.25_spmd, body=%wide.region_19.24_spmd.sunk | while | flops 482347136 | bytes 61189336 | solution.py:242
  835.9 5.7 gather_fusion.8
  901.5 5.7 gather_fusion.8
  964.2 5.3 copy.184
  971.9 129.8 %reduce-scatter.15.cloned.1.call-done = f32[128,128]{0,1:T(8,128)} async-done(((f32[8192,128]{0,1:T(8,128)}), f32[128,128]{0,1:T(8,128)}) %reduce-scatter.15.cloned.1.call-update) | async-done | bytes 65552 | tf_op jit(solution)/shard_map/reduce_scatter | solution.py:264
  1102.8 145.3 %reduce-scatter.13.cloned.1.call-done = f32[128,128]{0,1:T(8,128)} async-done(((f32[8192,128]{0,1:T(8,128)}), f32[128,128]{0,1:T(8,128)}) %reduce-scatter.13.cloned.1.call-update) | async-done | bytes 65552 | tf_op jit(solution)/shard_map/reduce_scatter | solution.py:261
  1253.0 20.9 %reduce-scatter.11.cloned.1.call-done = f32[256,128]{1,0:T(8,128)} async-done(((f32[256,512]{1,0:T(8,128)}), f32[256,128]{1,0:T(8,128)}) %reduce-scatter.11.cloned.1.call-update) | async-done | bytes 131088 | tf_op jit(solution)/shard_map/reduce_scatter | solution.py:271
  1275.5 187.6 %all-reduce.5.cloned.1.call-done = f32[4,512,128]{1,2,0:T(8,128)} async-done(((f32[4,512,128]{1,2,0:T(8,128)}), f32[4,512,128]{1,2,0:T(8,128)}) %all-reduce.5.cloned.1.call-update) | async-done | bytes 1048592 | tf_op jit(solution)/shard_map/psum | solution.py:274
  1465.7 20.8 %reduce-scatter.17.cloned.1.call-done = f32[128,128]{1,0:T(8,128)} async-done(((f32[128,512]{1,0:T(8,128)}), f32[128,128]{1,0:T(8,128)}) %reduce-scatter.17.cloned.1.call-update) | async-done | bytes 65552 | tf_op jit(solution)/shard_map/reduce_scatter | solution.py:272
  (274 shorter events, 272.4 us)
Async XLA Ops:
  7.2 39.4 %copy-start = (bf16[512,128]{1,0:T(8,128)(2,1)S(1)}, bf16[512,128]{1,0:T(8,128)(2,1)}, u32[]{:S(2)}) copy-start(bf16[512,128]{1,0:T(8,128)(2,1)} %param.18) | copy-start | bytes 393220
  19.1 15.3 %copy-start.8 = (bf16[128,512]{1,0:T(8,128)(2,1)}, bf16[128,512]{1,0:T(8,128)(2,1)S(1)}, u32[]{:S(2)}) copy-start(bf16[128,512]{1,0:T(8,128)(2,1)S(1)} %all_gather.16) | copy-start | bytes 393220
  22.2 12.2 copy-start.16
  22.2 13.1 copy-start.28
  22.2 62.9 %all-to-all-start = ((bf16[64,128,128]{1,2,0:T(8,128)(2,1)}), bf16[64,128,128]{1,2,0:T(8,128)(2,1)S(1)}, u32[]{:S(2)}, u32[]{:S(2)}) async-start(bf16[64,128,128]{1,2,0:T(8,128)(2,1)} %stack.12), calls=%async_computation | async-start | bytes 4194304 | tf_op jit(solution)/shard_map/all_to_all | solution.py:53
  34.4 84.1 %all-gather.4.cloned.1.call-start = ((), (), s32[]{:S(2)}) async-start(), calls=%async_computation.7 | async-start | bytes 2129920 | tf_op jit(solution)/shard_map/all_gather | solution.py:61
  35.3 253.2 %all-reduce.3.cloned.1.call-start = ((), (), s32[]{:S(2)}) async-start(), calls=%async_computation.8 | async-start | bytes 131072 | tf_op jit(solution)/shard_map/pmax | solution.py:101
  46.6 70.0 %copy-start.6 = (bf16[256,512]{1,0:T(8,128)(2,1)}, bf16[256,512]{1,0:T(8,128)(2,1)S(1)}, u32[]{:S(2)}) copy-start(bf16[256,512]{1,0:T(8,128)(2,1)S(1)} %all_gather.15) | copy-start | bytes 786436
  92.6 24.0 %copy-start.13 = (bf16[512,128]{1,0:T(8,128)(2,1)S(1)}, bf16[512,128]{1,0:T(8,128)(2,1)}, u32[]{:S(2)}) copy-start(bf16[512,128]{1,0:T(8,128)(2,1)} %param.19) | copy-start | bytes 393220
  116.6 385.4 %reduce-scatter.19.cloned.1.call-start = ((), (), s32[]{:S(2)}) async-start(), calls=%async_computation.17 | async-start | bytes 4259840
  361.2 287.0 %reduce-scatter.9.cloned.1.call-start = ((), (), s32[]{:S(2)}) async-start(), calls=%async_computation.9 | async-start | bytes 4259840 | tf_op jit(solution)/shard_map/reduce_scatter | solution.py:148
  371.1 279.3 %copy-start.21 = (bf16[256,128]{1,0:T(8,128)(2,1)S(1)}, bf16[256,128]{1,0:T(8,128)(2,1)}, u32[]{:S(2)}) copy-start(bf16[256,128]{1,0:T(8,128)(2,1)} %param.22) | copy-start | bytes 196612
  371.1 351.9 %all-gather.6.cloned.1.call-start = ((), (), s32[]{:S(2)}) async-start(), calls=%async_computation.10 | async-start | bytes 2129920 | tf_op jit(solution)/shard_map/all_gather | solution.py:162
  649.7 148.0 %all-gather.8.cloned.1.call-start = ((), (), s32[]{:S(2)}) async-start(), calls=%async_computation.11 | async-start | bytes 2129920 | tf_op jit(solution)/shard_map/all_gather | solution.py:163
  650.3 451.5 %reduce-scatter.15.cloned.1.call-start = ((), (), s32[]{:S(2)}) async-start(), calls=%async_computation.14 | async-start | bytes 4259840 | tf_op jit(solution)/shard_map/reduce_scatter | solution.py:264
  650.7 149.8 %copy-start.11 = (bf16[2,128,2,64]{1,0,3,2:T(2,128)(2,1)}, bf16[2,128,2,64]{1,0,3,2:T(2,128)(2,1)S(1)}, u32[]{:S(2)}) copy-start(bf16[2,128,2,64]{1,0,3,2:T(2,128)(2,1)S(1)} %copy.104) | copy-start | bytes 196612
  959.6 288.6 %reduce-scatter.13.cloned.1.call-start = ((), (), s32[]{:S(2)}) async-start(), calls=%async_computation.13 | async-start | bytes 4259840 | tf_op jit(solution)/shard_map/reduce_scatter | solution.py:261
  969.5 304.5 %reduce-scatter.11.cloned.1.call-start = ((), (), s32[]{:S(2)}) async-start(), calls=%async_computation.12 | async-start | bytes 655360 | tf_op jit(solution)/shard_map/reduce_scatter | solution.py:271
  969.6 132.2 %copy-start.9 = (bf16[128,512]{1,0:T(8,128)(2,1)S(1)}, bf16[128,512]{1,0:T(8,128)(2,1)}, u32[]{:S(2)}) copy-start(bf16[128,512]{1,0:T(8,128)(2,1)} %copy-done.8) | copy-start | bytes 393220
  971.5 491.7 %all-reduce.5.cloned.1.call-start = ((), (), s32[]{:S(2)}) async-start(), calls=%async_computation.16 | async-start | bytes 2097152 | tf_op jit(solution)/shard_map/psum | solution.py:274
  971.9 278.4 %copy-start.15 = (bf16[512,128]{1,0:T(8,128)(2,1)S(1)}, bf16[512,128]{1,0:T(8,128)(2,1)}, u32[]{:S(2)}) copy-start(bf16[512,128]{1,0:T(8,128)(2,1)} %param.20) | copy-start | bytes 393220
  1102.8 147.8 %copy-start.17 = (bf16[512,128]{1,0:T(8,128)(2,1)S(1)}, bf16[512,128]{1,0:T(8,128)(2,1)}, u32[]{:S(2)}) copy-start(bf16[512,128]{1,0:T(8,128)(2,1)} %param.21) | copy-start | bytes 393220
  1102.8 147.8 %copy-start.22 = (f32[128,128]{0,1:T(8,128)S(1)}, f32[128,128]{0,1:T(8,128)}, u32[]{:S(2)}) copy-start(f32[128,128]{0,1:T(8,128)} %reduce-scatter.15.cloned.1.call-done) | copy-start | bytes 196612
  1250.3 236.2 %reduce-scatter.17.cloned.1.call-start = ((), (), s32[]{:S(2)}) async-start(), calls=%async_computation.15 | async-start | bytes 327680 | tf_op jit(solution)/shard_map/reduce_scatter | solution.py:272
  (30 other events, 60.7 us)
Sparse Core Ops, SparseCore 0:
  38.6 79.8 all-gather.3
  122.5 165.9 all-reduce.2
  361.3 140.6 reduce-scatter.18
  506.0 142.1 reduce-scatter.8
  651.5 71.4 all-gather.5
  726.3 71.3 all-gather.7
  959.7 142.0 reduce-scatter.14
  1105.9 142.1 reduce-scatter.12
  1250.8 23.1 reduce-scatter.10
  1278.2 184.9 all-reduce.4
  1465.7 20.7 reduce-scatter.16
